TPU v7x, 256 devices: a whole 4x4x8 slice. The times are simulated.
256 devices in a mesh: wide: 64 (over x_lo, y, z), narrow: 4 (over x_hi, core).
Axes of the slice: x: 4 (x_hi: 2, x_lo: 2; x = x_hi * 2 + x_lo), y: 4, z: 8, core: 2. Of those that a mesh axis runs over, the one named last changes fastest.
Arguments:
- query_in: bfloat16 [8, 32, 14336], P(None, None, 'narrow'), may hold values from -1.0546875 to 1.0546875
- query_out: bfloat16 [8, 32, 4096], replicated, may hold values from -6 to 6
- train_in: bfloat16 [64, 32, 14336], P('wide', None, 'narrow'), may hold values from -6 to 6
- train_out: bfloat16 [64, 32, 4096], P('wide'), may hold values from -6 to 6
- basis_in: bfloat16 [14336, 14336], P('wide', 'narrow'), may hold values from -0.046875 to 0.046875
- basis_out: bfloat16 [4096, 4096], P('narrow', 'wide'), may hold values from -0.09375 to 0.09375
- eigvals: float32 [4096, 14336], P('narrow', 'wide'), may hold values from 0.02 to 40
Outputs:
- precond: bfloat16 [8, 4096, 14336], P(None, 'narrow', 'wide')
- scores: float32 [8, 64], replicated
All inputs are finite; a program needn't handle non-finite values.
Results may differ from a plain program's by a relative error of at most 0.0057.
Values may be sent and summed in bfloat16 or wider, within the bound.
A program may use at most 128 MiB of HBM per device.

v0:
```python
import jax
import jax.numpy as jnp
from jax import lax
from jax.sharding import PartitionSpec as P

DS = 4096
DA = 14336
RANK = 32


def contract_last(left_rows, right_rows):
    return lax.dot_general(
        left_rows, right_rows, (((1,), (1,)), ((), ())), preferred_element_type=jnp.float32
    )


def shards(query_in, query_out, train_in, train_out, basis_in, basis_out, eigvals):
    rank = train_in.shape[1]
    qrank = query_in.shape[1]
    queries = query_in.shape[0]
    small_side = query_out.shape[2]
    eig_total = lax.psum(jnp.sum(eigvals), ("wide", "narrow"))
    damping = 0.1 * eig_total / (DS * DA)

    def rotate_in(factors):
        flattened = factors.reshape(factors.shape[0] * factors.shape[1], factors.shape[2])
        product = contract_last(flattened, basis_in)
        return product.reshape(factors.shape[0], factors.shape[1], basis_in.shape[0])

    train_part = rotate_in(lax.all_gather(train_in, "wide", axis=0, tiled=True))
    query_part = rotate_in(query_in)
    train_sum, query_sum = lax.psum((train_part, query_part), "narrow")
    train_rot = train_sum.astype(jnp.bfloat16)
    query_rot = query_sum.astype(jnp.bfloat16)
    train_total = train_rot.shape[0]
    train_rows = train_total * rank
    query_left = query_out.reshape(queries * qrank, small_side)
    sample_cols = lax.all_to_all(train_out, "wide", split_axis=2, concat_axis=0, tiled=True)
    col_width = basis_out.shape[1]
    query_cols = lax.dynamic_slice_in_dim(
        query_left, lax.axis_index("wide") * col_width, col_width, 1
    )
    left_all = jnp.concatenate([sample_cols.reshape(train_rows, col_width), query_cols], 0)
    shares = lax.psum_scatter(
        contract_last(left_all, basis_out), "wide", scatter_dimension=0, tiled=True
    )
    rotated = lax.all_gather(shares.astype(jnp.bfloat16), "wide", axis=0, tiled=True)
    train_side = rotated[:train_rows]
    query_side = rotated[train_rows:]
    query_side = query_side.reshape(queries, qrank, basis_out.shape[0])
    product = jnp.einsum("qki,qkj->qij", query_side, query_rot, preferred_element_type=jnp.float32)
    precond = (product / (eigvals + damping)).astype(jnp.bfloat16)
    train_flat = train_rot.reshape(train_rows, basis_in.shape[0])
    side_wide = train_side.astype(jnp.float32)
    local_scores = []
    for query_pos in range(queries):
        projected = contract_last(train_flat, precond[query_pos])
        per_pair = jnp.sum(projected * side_wide, axis=1)
        local_scores.append(jnp.sum(per_pair.reshape(train_total, rank), axis=1))
    stacked = jnp.stack(local_scores, 0)
    summed_scores = lax.psum(stacked, ("wide", "narrow"))
    scores = summed_scores / jnp.sqrt(jnp.float32(RANK * DS * DA))
    return (precond, scores)


def solution(mesh):
    placed = (
        P(None, None, "narrow"),
        P(),
        P("wide", None, "narrow"),
        P("wide", None, None),
        P("wide", "narrow"),
        P("narrow", "wide"),
        P("narrow", "wide"),
    )
    return jax.shard_map(
        shards,
        mesh=mesh,
        in_specs=placed,
        out_specs=(P(None, "narrow", "wide"), P()),
        check_vma=False,
    )
```

profile of v0, /device:TPU:1, one launch (start us, length us, event | category | flops | bytes accessed | tf_op | source)
XLA Modules:
  0.0 1088.7 jit_solution(1653564901491522614)
XLA Ops:
  7.2 5.2 copy.15
  12.4 0.5 broadcast.2
  12.9 23.4 %reduce = bf16[4096,32]{1,0:T(8,128)(2,1)S(1)} reduce(bf16[4096,1,32]{2,1,0:T(2,128)(2,1)} %bitcast.65, bf16[]{:T(256)} %broadcast.2), dimensions={1}, to_apply=%bitcast.47.reduce_sub_computation | reduce | bytes 524290
  36.3 1.7 reshape.66
  38.1 13.6 %all-to-all-start = ((bf16[64,2,1024]{2,1,0:T(2,128)(2,1)}), bf16[64,2,1024]{2,1,0:T(2,128)(2,1)S(1)}, u32[]{:S(2)}, u32[]{:S(2)}) async-start(bf16[64,2,1024]{2,1,0:T(2,128)(2,1)} %reshape.66), calls=%async_computation | async-start | bytes 524288 | tf_op jit(solution)/shard_map/all_to_all | solution.py:38
  51.8 11.4 %all-to-all-done = bf16[64,2,1024]{2,1,0:T(2,128)(2,1)S(1)} async-done(((bf16[64,2,1024]{2,1,0:T(2,128)(2,1)}), bf16[64,2,1024]{2,1,0:T(2,128)(2,1)S(1)}, u32[]{:S(2)}, u32[]{:S(2)}) %all-to-all-start) | async-done | bytes 262176 | tf_op jit(solution)/shard_map/all_to_all | solution.py:38
  63.2 1.4 reshape.67
  64.5 2.1 copy.16
  66.6 0.5 all_to_all.12
  67.1 0.3 copy.17
  67.5 5.0 fusion.13
  72.5 168.7 %fusion = f32[40,1024]{1,0:T(8,128)S(1)} fusion(f32[2304,1024]{1,0:T(8,128)} %fusion.13), kind=kCustom, calls=%all-reduce-scatter | all-reduce-scatter fusion | flops 2621441 | bytes 9602048
  241.2 1.3 collective-permute-start.1
  242.6 1.3 collective-permute-start.6
  243.9 1.3 collective-permute-start.2
  245.2 1.3 collective-permute-start.3
  246.5 1.3 collective-permute-start.4
  247.8 5.8 collective-permute-start.5
  253.6 3.9 collective-permute-start
  257.5 0.6 dynamic-slice.4
  258.8 0.3 collective-permute-done
  259.1 1.2 concatenate.4
  260.2 0.7 fusion.18
  260.9 0.2 all-gather.4.cloned.1.call-start
  261.1 0.5 all-gather.4.cloned.1.call-update
  261.7 0.8 reduce_sum.153
  262.5 114.0 %psum.29 = f32[]{:T(128)} all-reduce(f32[]{:T(128)} %reduce_sum.153), channel_id=1, replica_groups=mesh['wide'=64,'narrow'=4] {'wide','narrow'}, use_global_device_ids=true, to_apply=%region_3.0 | all-reduce | flops 1 | bytes 8 | tf_op jit(solution)/shard_map/psum | solution.py:22
  376.6 2.6 fusion.11
  379.9 183.2 %all-gather.6.cloned.1.call-done = bf16[64,36,1024]{2,1,0:T(8,128)(2,1)} async-done(((bf16[1,36,1024]{2,1,0:T(8,128)(2,1)}), bf16[64,36,1024]{2,1,0:T(8,128)(2,1)}) %all-gather.6.cloned.1.call-update) | async-done | bytes 4718608 | tf_op jit(solution)/shard_map/all_gather | solution.py:47
  563.2 7.2 reshape.63
  570.4 4.7 slice.42
  575.1 6.4 copy.19
  581.5 310.4 %all-gather.4.cloned.1.call-done = bf16[64,32,3584]{2,1,0:T(8,128)(2,1)} async-done(((bf16[1,32,3584]{2,1,0:T(8,128)(2,1)}), bf16[64,32,3584]{2,1,0:T(8,128)(2,1)}) %all-gather.4.cloned.1.call-update) | async-done | bytes 14680080 | tf_op jit(solution)/shard_map/all_gather | solution.py:30
  892.0 10.9 %fusion.9 = f32[64,32,224]{2,1,0:T(8,128)} fusion(bf16[64,32,3584]{2,1,0:T(8,128)(2,1)} %all-gather.4.cloned.1.call-done, bf16[224,3584]{1,0:T(8,128)(2,1)} %param.11), kind=kOutput, calls=%fused_computation.17 | convolution fusion | flops 3288334336 | bytes 18120704 | tf_op jit(solution)/shard_map/dot_general | solution.py:12
  902.9 88.0 %all-reduce.4 = (bf16[8,32,224]{2,1,0:T(8,128)(2,1)S(1)}, bf16[64,32,224]{2,1,0:T(8,128)(2,1)S(1)}) all-reduce(f32[8,32,224]{2,1,0:T(8,128)S(1)} %fusion.11, f32[64,32,224]{2,1,0:T(8,128)} %fusion.9), channel_id=1, replica_groups=mesh['wide'=64,'narrow'=4] {'narrow'}, use_global_device_ids=true, to_apply=%region_1.0 | all-reduce | flops 516096 | bytes 3096576 | tf_op jit(solution)/shard_map/psum | solution.py:32
  990.9 1.2 divide_convert_fusion
  992.1 1.2 copy-done.2
  993.3 1.3 fusion.8
  994.6 1.3 fusion.7
  995.9 1.3 fusion.6
  997.2 1.3 fusion.5
  998.5 1.3 fusion.4
  999.8 1.3 fusion.3
  1001.2 1.3 fusion.2
  1002.5 1.3 fusion.1
  1004.1 0.1 reduce_sum.157
  1005.4 75.9 %psum.31 = f32[8,64]{1,0:T(8,128)S(1)} all-reduce(f32[8,64]{1,0:T(8,128)S(1)} %stack.35), channel_id=1, replica_groups=mesh['wide'=64,'narrow'=4] {'wide','narrow'}, use_global_device_ids=true, to_apply=%region_21.0 | all-reduce | flops 512 | bytes 4096 | tf_op jit(solution)/shard_map/psum | solution.py:61
  1081.3 0.6 broadcast_multiply_fusion
  (43 shorter events, 1.7 us)
Async XLA Ops:
  7.2 44.5 %copy-start = (bf16[8,32,4096]{2,1,0:T(8,128)(2,1)S(1)}, bf16[8,32,4096]{2,1,0:T(8,128)(2,1)}, u32[]{:S(2)}) copy-start(bf16[8,32,4096]{2,1,0:T(8,128)(2,1)} %param.8) | copy-start | bytes 6291460
  36.3 31.2 %copy-start.4 = (bf16[1024,64]{0,1:T(8,128)(2,1)S(1)}, bf16[1024,64]{0,1:T(8,128)(2,1)}, u32[]{:S(2)}) copy-start(bf16[1024,64]{0,1:T(8,128)(2,1)} %param.12) | copy-start | bytes 393220
  38.1 25.1 %all-to-all-start = ((bf16[64,2,1024]{2,1,0:T(2,128)(2,1)}), bf16[64,2,1024]{2,1,0:T(2,128)(2,1)S(1)}, u32[]{:S(2)}, u32[]{:S(2)}) async-start(bf16[64,2,1024]{2,1,0:T(2,128)(2,1)} %reshape.66), calls=%async_computation | async-start | bytes 524288 | tf_op jit(solution)/shard_map/all_to_all | solution.py:38
  51.6 511.5 %all-gather.6.cloned.1.call-start = ((), (), s32[]{:S(2)}) async-start(), calls=%async_computation.2 | async-start | bytes 5324800 | tf_op jit(solution)/shard_map/all_gather | solution.py:47
  72.5 185.0 %copy-start.5 = (u32[256]{0:T(256)S(1)}, u32[256]{0:T(256)}, u32[]{:S(2)}) copy-start(u32[256]{0:T(256)} %constant.28) | copy-start | bytes 3076
  72.5 189.2 %copy-start.3 = (f32[1024,224]{0,1:T(8,128)S(1)}, f32[1024,224]{0,1:T(8,128)}, u32[]{:S(2)}) copy-start(f32[1024,224]{0,1:T(8,128)} %param.13) | copy-start | bytes 2752516
  241.2 12.3 %collective-permute-start.1 = (bf16[40,1024]{1,0:T(8,128)(2,1)S(1)}, bf16[40,1024]{1,0:T(8,128)(2,1)S(1)}, u32[]{:S(2)}, u32[]{:S(2)}) collective-permute-start(bf16[40,1024]{1,0:T(8,128)(2,1)S(1)} %convert.12), channel_id=1, source_target_pairs={{0,8},{4,12},{8,16},{12,20},{16,24},{20,28},{24,32},{28,36},{32,40... | collective-permute-start | bytes 245768
  242.6 5.2 collective-permute-start.6
  243.9 14.9 %collective-permute-start.2 = (bf16[40,1024]{1,0:T(8,128)(2,1)S(1)}, bf16[40,1024]{1,0:T(8,128)(2,1)S(1)}, u32[]{:S(2)}, u32[]{:S(2)}) collective-permute-start(bf16[40,1024]{1,0:T(8,128)(2,1)S(1)} %convert.12), channel_id=1, source_target_pairs={{0,12},{4,16},{8,20},{12,24},{16,28},{20,32},{24,36},{28,40},{32,4... | collective-permute-start | bytes 245768
  245.2 13.6 %collective-permute-start.3 = (bf16[40,1024]{1,0:T(8,128)(2,1)S(1)}, bf16[40,1024]{1,0:T(8,128)(2,1)S(1)}, u32[]{:S(2)}, u32[]{:S(2)}) collective-permute-start(bf16[40,1024]{1,0:T(8,128)(2,1)S(1)} %convert.12), channel_id=1, source_target_pairs={{0,16},{4,20},{8,24},{12,28},{16,32},{20,36},{24,40},{28,44},{32,4... | collective-permute-start | bytes 245768
  246.5 12.3 %collective-permute-start.4 = (bf16[40,1024]{1,0:T(8,128)(2,1)S(1)}, bf16[40,1024]{1,0:T(8,128)(2,1)S(1)}, u32[]{:S(2)}, u32[]{:S(2)}) collective-permute-start(bf16[40,1024]{1,0:T(8,128)(2,1)S(1)} %convert.12), channel_id=1, source_target_pairs={{0,20},{4,24},{8,28},{12,32},{16,36},{20,40},{24,44},{28,48},{32,5... | collective-permute-start | bytes 245768
  247.8 11.0 %collective-permute-start.5 = (bf16[40,1024]{1,0:T(8,128)(2,1)S(1)}, bf16[40,1024]{1,0:T(8,128)(2,1)S(1)}, u32[]{:S(2)}, u32[]{:S(2)}) collective-permute-start(bf16[40,1024]{1,0:T(8,128)(2,1)S(1)} %convert.12), channel_id=1, source_target_pairs={{0,24},{4,28},{8,32},{12,36},{16,40},{20,44},{24,48},{28,52},{32,5... | collective-permute-start | bytes 245768
  253.6 5.5 collective-permute-start
  260.9 631.0 %all-gather.4.cloned.1.call-start = ((), (), s32[]{:S(2)}) async-start(), calls=%async_computation.1 | async-start | bytes 14909440 | tf_op jit(solution)/shard_map/all_gather | solution.py:30
  581.5 409.4 %slice-start = ((bf16[2304,1024]{1,0:T(8,128)(2,1)}), bf16[256,1024]{1,0:T(8,128)(2,1)S(1)}, s32[]{:S(2)}) async-start(bf16[2304,1024]{1,0:T(8,128)(2,1)} %reshape.63), calls=%async_computation.3 | async-start | bytes 1048576 | tf_op jit(solution)/shard_map/slice | solution.py:49
  990.9 2.4 copy-start.2
  992.1 10.4 copy-start.6
  1001.1 80.7 %copy-start.1 = (bf16[8,32,4096]{2,1,0:T(8,128)(2,1)S(1)}, bf16[8,32,4096]{2,1,0:T(8,128)(2,1)}, u32[]{:S(2)}) copy-start(bf16[8,32,4096]{2,1,0:T(8,128)(2,1)} %param.8) | copy-start | bytes 6291460
Sparse Core Ops, SparseCore 0:
  261.0 302.0 all-gather.5
  565.0 326.9 all-gather.3
where the time goes:
time: 1090 us
  waiting for transfers between devices  506 us (46%)
  blocking collectives  447 us (41%)
  local copies, waits for them, and re-layouts  34.4 us (3%)
  matrix products  30.2 us (3%)
  starting transfers between devices  30 us (3%)
  other arithmetic  25.9 us (2%)
  between operations  15.8 us (1%)
    all_gather x1, waiting for transfers between devices, shards(): train_part = rotate_in(lax.all_gather(train_in, 'wide', axis=0, tiled=True))  310 us
    all_gather x1, waiting for transfers between devices, shards(): lax.all_gather(shares.astype(jnp.bfloat16), 'wide', axis=0, tiled=True)  183 us
    unnamed x1, blocking collectives  169 us
    psum x1, blocking collectives, shards(): eig_total = lax.psum(jnp.sum(eigvals), ('wide', 'narrow'))  114 us
    psum x1, blocking collectives, shards(): train_sum, query_sum = lax.psum((train_part, query_part), 'narrow')  88 us
    psum x1, blocking collectives, shards(): summed_scores = lax.psum(stacked, ('wide', 'narrow'))  75.9 us
    dot_general x11, matrix products, contract_last(): lax.dot_general(left_rows, right_rows, (((1,), (1,)), ((), ())), preferre...  29 us
    unnamed x24, local copies, waits for them, and re-layouts  26 us
  transfers between devices with their start and end apart: 10, of which 4 were waited for; matrix products, arithmetic and copies ran while one was open for 2% of the time, Pallas kernels for 0%

commit v1 on v0

v1 whole, which is shorter than its diff:
```python
import jax
import jax.numpy as jnp
from jax import lax
from jax.experimental import pallas as pl
from jax.experimental.pallas import tpu as pltpu
from jax.sharding import PartitionSpec as P

DS = 4096
DA = 14336
RANK = 32
Y = 4
Z = 8
X = 4
GROUP = 8
MESH = pl.DeviceIdType.MESH
VMEM = pl.BlockSpec(memory_space=pltpu.VMEM)
ANY = pl.BlockSpec(memory_space=pl.ANY)


class Place:
    def __init__(self):
        wide = lax.axis_index("wide")
        narrow = lax.axis_index("narrow")
        self.z = lax.rem(wide, Z)
        self.y = lax.rem(wide // Z, Y)
        self.x_lo = wide // (Y * Z)
        self.x_hi = narrow // 2
        self.core = lax.rem(narrow, 2)
        self.n = narrow
        self.x = self.x_hi * 2 + self.x_lo
        self.g = self.x * 2 + self.core

    def dev(self, x_hi=None, x_lo=None, core=None, y=None, z=None):
        x_hi = self.x_hi if x_hi is None else x_hi
        x_lo = self.x_lo if x_lo is None else x_lo
        core = self.core if core is None else core
        y = self.y if y is None else y
        z = self.z if z is None else z
        return ((x_lo * Y + y) * Z + z, x_hi * 2 + core)

    def in_group(self, g):
        return self.dev(x_hi=g // 4, x_lo=lax.rem(g // 2, 2), core=lax.rem(g, 2))


def step(value, by, size):
    return lax.rem(value + (by % size), size)


def greet(devices):
    barrier = pltpu.get_barrier_semaphore()
    for device in devices:
        pl.semaphore_signal(barrier, inc=1, device_id=device, device_id_type=MESH)
    return lambda: pl.semaphore_wait(barrier, len(devices))


class Net:
    def __init__(self, me, send_sems, recv_sems):
        self.me = me
        self.send_sems = send_sems
        self.recv_sems = recv_sems
        self.sent = 0
        self.keys = {}
        self.pending = []

    def sem(self, key):
        return self.recv_sems.at[self.keys.setdefault(key, len(self.keys))]

    def send(self, src, dst, to, key, when=None):
        copy = pltpu.make_async_remote_copy(
            src_ref=src, dst_ref=dst, send_sem=self.send_sems.at[self.sent],
            recv_sem=self.sem(key), device_id=to, device_id_type=MESH,
        )
        self.sent += 1
        if when is None:
            copy.start()
        else:
            pl.when(when)(copy.start)
        self.pending.append((when, copy))
        return copy

    def arrive(self, dst, key, when=None):
        copy = pltpu.make_async_remote_copy(
            src_ref=dst, dst_ref=dst, send_sem=self.send_sems.at[0], recv_sem=self.sem(key),
            device_id=self.me.dev(core=1 - self.me.core), device_id_type=MESH,
        )
        if when is None:
            copy.wait_recv()
        else:
            pl.when(when)(copy.wait_recv)

    def finish(self):
        for when, copy in self.pending:
            if when is None:
                copy.wait_send()
            else:
                pl.when(when)(copy.wait_send)


def ups(size, odd):
    return size // 2 if odd == 0 else size - 1 - size // 2


class Gather:
    def __init__(self, net, name, buf, slot, relative=False):
        self.net, self.name, self.buf, self.slot, self.relative = net, name, buf, slot, relative

    def send(self, axis, back_y, back_z, way):
        net, me = self.net, self.net.me
        src = self.buf.at[self.slot(back_y, back_z)]
        if axis == "y":
            key = (self.name, (back_y + way) % Y, back_z % Z)
            net.send(src, src, me.dev(y=step(me.y, way, Y)), key)
        else:
            dst = self.buf.at[self.slot(back_y, back_z + way)] if self.relative else src
            key = (self.name, back_y % Y, (back_z + way) % Z)
            net.send(src, dst, me.dev(z=step(me.z, way, Z)), key)

    def arrive(self, back_y, back_z):
        key = (self.name, back_y % Y, back_z % Z)
        self.net.arrive(self.buf.at[self.slot(back_y, back_z)], key)

    def ring(self, axis, fixed, far, odd):
        size = Y if axis == "y" else Z
        up = ups(size, odd % 2)
        for way, reach in ((1, up), (-1, size - 1 - up)):
            if far > reach:
                continue
            at = (far * way, fixed) if axis == "y" else (fixed, far * way)
            if far > 0:
                self.arrive(*at)
            if far < reach:
                self.send(axis, *at, way)

    def direct_y(self):
        for back in range(1, Y):
            self.send("y", 0, 0, back)


class PairShare:
    def __init__(self, net, name, src, dst, parts):
        self.net, self.name, self.src, self.dst = net, name, src, dst
        self.half = src.shape[0] // 2
        self.width = src.shape[1] // parts
        self.parts = parts
        me = net.me
        self.home = me.x_lo == me.core
        self.away = me.x_lo != me.core
        self.relayed = []

    def rows(self, which):
        return pl.ds(which * self.half, self.half)

    def columns(self, part):
        return slice(part * self.width, part * self.width + self.width)

    def start(self, part):
        me, net = self.net.me, self.net
        columns = self.columns(part)
        for core in range(2):
            net.send(
                self.src.at[self.rows(core), columns],
                self.dst.at[me.x_lo, self.rows(core), columns],
                me.dev(x_lo=1 - me.x_lo, core=core), (self.name, part, 0), when=self.away,
            )
        net.send(
            self.src.at[:, columns], self.dst.at[me.x_lo, :, columns],
            me.dev(core=1 - me.core), (self.name, part, 1), when=self.home,
        )

    def relay(self, part):
        me, net = self.net.me, self.net
        block = self.dst.at[1 - me.x_lo, self.rows(me.core), self.columns(part)]
        net.arrive(block, (self.name, part, 0))
        self.relayed.append(net.send(block, block, me.dev(core=1 - me.core), (self.name, part, 2)))
        net.pending.pop()

    def end(self):
        me, net = self.net.me, self.net
        for part in range(self.parts):
            columns = self.columns(part)
            other = self.dst.at[1 - me.x_lo, self.rows(1 - me.core), columns]
            net.arrive(other, (self.name, part, 2))
            whole = self.dst.at[me.x_lo, :, columns]
            net.arrive(whole, (self.name, part, 1), when=self.away)
        for copy in self.relayed:
            copy.wait_send()


def position(back_z):
    back_z = back_z % Z
    return 2 * back_z - (back_z > 0) if back_z <= Z // 2 else 2 * (Z - back_z)


def nt(a, b):
    return lax.dot_general(a, b, (((1,), (1,)), ((), ())), preferred_element_type=jnp.float32)


def tn_t(a, b):
    return lax.dot_general(a, b, (((0,), (1,)), ((), ())), preferred_element_type=jnp.float32)


def spread_group(net, name, buf):
    mine = buf.at[net.me.g]
    for back in range(1, GROUP):
        net.send(mine, mine, net.me.in_group(step(net.me.g, back, GROUP)), (name, back))


def collect_group(net, name, buf):
    for back in range(1, GROUP):
        net.arrive(buf.at[step(net.me.g, -back, GROUP)], (name, back))


def spread_y(net, name, buf):
    mine = buf.at[net.me.y]
    for back in range(1, Y):
        net.send(mine, mine, net.me.dev(y=step(net.me.y, back, Y)), (name, back))


def collect_y(net, name, buf):
    for back in range(1, Y):
        net.arrive(buf.at[step(net.me.y, -back, Y)], (name, back))


def spread_z(net, name, buf):
    mine = buf.at[net.me.z]
    for back in range(1, Z):
        net.send(mine, mine, net.me.dev(z=step(net.me.z, back, Z)), (name, back))


def collect_z(net, name, buf):
    for back in range(1, Z):
        net.arrive(buf.at[step(net.me.z, -back, Z)], (name, back))


def rotate_kernel(
    train, basis, eigs, train_out, small, query_in, query_out,
    out_side, qr, eig_sum, part_sum,
    tr, sides, eigs_all, eigs_round, inverse, outer_own, outer,
    scaled, ts, pairs, f1, f2, f3,
    train_all, basis_all, outer_all, small_all, small_pad,
    basis_own, query_rows, query_cols, eigs_own,
    cpart, c_in, st, s_in, sq, sq_in, qp, qp_in, e1, e2, e3,
    send_sems, recv_sems, local_sems,
):
    bf16, f32 = jnp.bfloat16, jnp.float32
    me = Place()
    net = Net(me, send_sems, recv_sems)
    home = me.x_lo == me.core
    away = me.x_lo != me.core
    swapped = dict(x_lo=me.core, core=me.x_lo)

    loads = [
        pltpu.make_async_copy(train_out, outer_own, local_sems.at[8 + 2 * Y]),
        pltpu.make_async_copy(eigs, eigs_own, local_sems.at[5]),
        pltpu.make_async_copy(basis, basis_own, local_sems.at[6]),
        pltpu.make_async_copy(query_in, query_rows, local_sems.at[7]),
    ]
    cols_z = me.z // 2 * 128
    for part in range(2 * Y):
        offset = pl.multiple_of(part * (query_out.shape[1] // (2 * Y)) + cols_z, 128)
        loads.append(
            pltpu.make_async_copy(
                query_out.at[:, pl.ds(offset, 128)],
                query_cols.at[:, part * 128 : part * 128 + 128],
                local_sems.at[8 + part],
            )
        )
    for load in loads:
        load.start()
    partners = []
    for back in range(Y):
        for flip_x in range(2):
            for flip_core in range(2):
                if back + flip_x + flip_core > 0:
                    partners.append(
                        me.dev(
                            x_lo=1 - me.x_lo if flip_x else me.x_lo,
                            core=1 - me.core if flip_core else me.core,
                            y=step(me.y, back, Y),
                        )
                    )
    for back in range(1, Z):
        partners.append(me.dev(z=step(me.z, back, Z), **swapped))
        partners.append(me.dev(z=step(me.z, back, Z)))
    for x_lo in range(2):
        for core in range(2):
            partners.append(me.dev(x_hi=1 - me.x_hi, x_lo=x_lo, core=core))
    all_here = greet(partners)
    small_pad[...] = jnp.zeros_like(small_pad)
    loads[0].wait()
    depth = small.shape[0]
    for z in range(Z):
        pieces = []
        for part in range(2 * Y):
            first = (part * Z + z) * depth
            pieces.append(outer_own[:, first : first + depth])
        outer[z] = jnp.concatenate(pieces, axis=1)
    all_here()

    own_slot = train_all.at[0, me.y]
    own_copy = pltpu.make_async_copy(train, own_slot, local_sems.at[0])
    pl.when(home)(own_copy.start)
    net.send(train, own_slot, me.dev(**swapped), "swap", when=away)

    outer_slot = outer_all.at[me.z, me.y]
    outer_copy = pltpu.make_async_copy(outer.at[me.z], outer_slot, local_sems.at[1])
    pl.when(home)(outer_copy.start)
    net.send(outer.at[me.z], outer_slot, me.dev(**swapped), ("outer", 0), when=away)
    for back in range(1, Z):
        to_z = step(me.z, back, Z)
        net.send(outer.at[to_z], outer_slot, me.dev(z=to_z, **swapped), ("outer", back))

    width = small.shape[1] // Y
    small_slot = me.x_lo * Y + me.y

    def small_part(y):
        return small.at[:, pl.ds(pl.multiple_of(y * width, width), width)]

    small_copy = pltpu.make_async_copy(small_part(me.y), small_all.at[small_slot], local_sems.at[2])
    pl.when(home)(small_copy.start)
    for back in range(Y):
        to_y = step(me.y, back, Y)
        for core in range(2):
            pair = net.keys.setdefault(("small", back, 0), len(net.keys))
            other = net.keys.setdefault(("small", back, 1), len(net.keys))
            copy = pltpu.make_async_remote_copy(
                src_ref=small_part(to_y), dst_ref=small_all.at[small_slot],
                send_sem=net.send_sems.at[net.sent],
                recv_sem=net.recv_sems.at[pair + (other - pair) * me.x_lo],
                device_id=me.dev(x_lo=me.core, core=core, y=to_y), device_id_type=MESH,
            )
            net.sent += 1
            when = None
            if back == 0:
                when = jnp.logical_or(away, me.core != core)
                pl.when(when)(copy.start)
            else:
                copy.start()
            net.pending.append((when, copy))

    rows_q = qp.shape[0] // 4
    loads[1].wait()
    tile = jnp.sum(eigs_own[...].reshape(-1, 8, eigs_own.shape[1]), axis=0)
    e1[me.g] = sum(tile[:, 128 * part : 128 * part + 128] for part in range(tile.shape[1] // 128))
    spread_group(net, "e1", e1)
    eigs_round[...] = eigs_own[...].astype(bf16)

    pl.when(home)(own_copy.wait)
    net.arrive(own_slot, "swap", when=away)
    trains = Gather(
        net, "train", train_all,
        lambda back_y, back_z: (position(back_z), step(me.y, -back_y, Y)), relative=True,
    )

    def groups(far):
        return (far,) if far in (0, Z // 2) else (far, -far)

    def train_z(far):
        trains.ring("z", 0, far, 0)
        for back_z in groups(far):
            trains.ring("y", back_z, 0, back_z)

    def train_y(far):
        for hop in range(1, Y // 2 + 1):
            for back_z in groups(far):
                trains.ring("y", back_z, hop, back_z)

    def side_z(far):
        for back in range(Y):
            smalls.ring("z", back, far, back)

    train_z(0)
    share_basis = PairShare(net, "basis", basis, basis_all, 4)
    share_eigs = PairShare(net, "eigs", eigs_round, eigs_all, 1)

    def outer_rows():
        pl.when(home)(outer_copy.wait)
        net.arrive(outer_slot, ("outer", 0), when=away)
        for back in range(1, Z):
            net.arrive(outer_all.at[step(me.z, -back, Z), me.y], ("outer", back))
        block = outer_all.at[:, me.y]
        for back in range(1, Y):
            net.send(block, block, me.dev(y=step(me.y, back, Y)), ("outer_y", back))

    def query_parts():
        loads[2].wait()
        loads[3].wait()
        qp[...] = nt(basis_own[...], query_rows[...])
        for back in range(1, 4):
            to_n = step(me.n, back, 4)
            net.send(
                qp.at[pl.ds(to_n * rows_q, rows_q)], qp_in.at[back],
                me.dev(x_hi=to_n // 2, core=lax.rem(to_n, 2)), ("qp", back),
            )

    def place_own():
        @pl.when(home)
        def _():
            basis_all[me.x_lo] = basis_own[...]
            eigs_all[me.x_lo] = eigs_round[...]

    rows_s = st.shape[0] // Z
    cols = st.shape[1]

    def side_parts():
        pl.when(home)(small_copy.wait)
        for x_lo in range(2):
            for back in range(Y):
                slot = small_all.at[x_lo * Y + step(me.y, -back, Y)]
                if back == 0:
                    here = jnp.logical_and(home, me.x_lo == x_lo)
                    net.arrive(slot, ("small", back, x_lo), when=jnp.logical_not(here))
                else:
                    net.arrive(slot, ("small", back, x_lo))
        for load in loads[4:]:
            load.wait()
        pad_row = lax.rem(me.z, 2) * depth
        for part in range(2 * Y):
            at = pl.ds(pl.multiple_of(part * 128 + pad_row, depth), depth)
            small_pad[at, :] = small_all[part]
        sq[...] = tn_t(small_pad[...], query_cols[...])
        for back in range(1, Z):
            to_z = step(me.z, back, Z)
            part = pl.ds(pl.multiple_of(to_z * rows_s, rows_s), rows_s)
            net.send(sq.at[part], sq_in.at[back], me.dev(z=to_z), ("side_q", back))
        for back in range(1, Y):
            net.arrive(outer_all.at[:, step(me.y, -back, Y)], ("outer_y", back))
        st[...] = tn_t(
            small_all[...].reshape(-1, width), outer_all[...].reshape(-1, 2 * Y * depth)
        ).astype(bf16)
        for back in range(1, Z):
            to_z = step(me.z, back, Z)
            part = pl.ds(pl.multiple_of(to_z * rows_s, rows_s), rows_s)
            net.send(st.at[part], s_in.at[back], me.dev(z=to_z), ("side", back))

    def query_sums():
        part = pl.ds(me.n * rows_q, rows_q)
        total = qp[part]
        for back in range(1, 4):
            net.arrive(qp_in.at[back], ("qp", back))
            total += qp_in[back]
        qr[me.x_lo, part] = total
        mine = qr.at[me.x_lo, part]
        for back in range(1, GROUP):
            net.send(mine, mine, me.in_group(step(me.g, back, GROUP)), ("qr", back))

    def side_sums():
        part = pl.ds(pl.multiple_of(me.z * rows_s, rows_s), rows_s)
        total = st[part].astype(f32)
        total_q = sq[part]
        for back in range(1, Z):
            net.arrive(sq_in.at[back], ("side_q", back))
            total_q += sq_in[back]
            net.arrive(s_in.at[back], ("side", back))
            total += s_in[back].astype(f32)
        sides[me.y, me.z, :, :cols] = total.astype(bf16)
        sides[me.y, me.z, :, cols:] = total_q.astype(bf16)

    smalls = Gather(
        net, "sides", sides,
        lambda back_y, back_z: (step(me.y, -back_y, Y), step(me.z, -back_z, Z)),
    )
    rows_c = cpart.shape[0] // X
    rows_g = Y * train.shape[0]

    def lanes(batch):
        low, high = (0, 1) if batch == 0 else (2 * batch - 1, min(2 * batch + 1, Z))
        return low, high, slice(low * rows_g, high * rows_g)

    def x_part(x):
        return pl.ds(pl.multiple_of(x * rows_c, rows_c), rows_c)

    def to_x(back):
        x = step(me.x, back, X)
        return x, me.dev(x_hi=x // 2, x_lo=lax.rem(x, 2))

    def multiply(batch):
        low, high, span = lanes(batch)
        rows = train_all[low:high].reshape((high - low) * rows_g, train.shape[1])
        both = basis_all[...].reshape(-1, train.shape[1])
        cpart[:, span] = nt(both, rows).astype(bf16)
        for back in range(1, X):
            x, device = to_x(back)
            net.send(
                cpart.at[x_part(x), span], c_in.at[back, :, span], device, ("ct", batch, back)
            )

    def combine(batch):
        span = lanes(batch)[2]
        part = x_part(me.x)
        total = cpart[part, span].astype(f32)
        for back in range(1, X):
            net.arrive(c_in.at[back, :, span], ("ct", batch, back))
            total += c_in[back, :, span].astype(f32)
        tr[part, span] = total.astype(bf16)
        mine = tr.at[part, span]
        for back in range(1, X):
            net.send(mine, mine, to_x(back)[1], ("tr", batch, back))

    def swap_queries(far):
        for back_z in groups(far):
            z = step(me.z, -back_z, Z)
            net.send(
                sides.at[:, z, :, cols:], out_side.at[:, z], me.dev(**swapped),
                ("swap_q", back_z % Z), when=away,
            )

    def score(batches):
        for batch in batches:
            for back in range(1, X):
                part = x_part(step(me.x, -back, X))
                net.arrive(tr.at[part, lanes(batch)[2]], ("tr", batch, back))
        span = slice(lanes(batches[0])[2].start, lanes(batches[-1])[2].stop)

        def one(query, carry):
            projected = jnp.dot(scaled[query], ts[:, span], preferred_element_type=f32)
            product = projected * tr[:, span].astype(f32)
            pairs[query, :, span] = jnp.sum(product.reshape(-1, 8, product.shape[1]), axis=0)
            return carry

        lax.fori_loop(0, pairs.shape[0], one, 0, unroll=2)

    def pick(block, query):
        lane = lax.broadcasted_iota(jnp.int32, block.shape, 1)
        keep = jnp.logical_and(lane >= query * RANK, lane < (query + 1) * RANK)
        return jnp.where(keep, block, 0.0).astype(bf16)

    def scale(query, carry):
        left = pick(qr[...].reshape(-1, qr.shape[2]), query)
        product = nt(left, sides[:, :, :, cols:].reshape(-1, qr.shape[2]))
        scaled[query] = (product * inverse[...].reshape(product.shape)).astype(bf16)
        return carry

    outer_rows()
    share_basis.start(0)
    train_z(1)
    query_parts()
    train_z(2)
    side_parts()
    train_z(3)
    share_basis.start(1)
    query_sums()
    collect_group(net, "e1", e1)
    e2[me.y] = jnp.sum(e1[...], axis=0)
    spread_y(net, "e2", e2)
    train_z(4)
    share_basis.start(2)
    share_basis.start(3)
    side_sums()
    smalls.direct_y()
    smalls.ring("z", 0, 0, 0)
    place_own()
    train_y(0)
    share_eigs.start(0)
    for back in range(1, Y):
        smalls.arrive(back, 0)
        smalls.ring("z", back, 0, back)
    swap_queries(0)
    train_y(1)
    side_z(1)
    swap_queries(1)
    share_basis.relay(0)
    share_basis.relay(1)
    collect_y(net, "e2", e2)
    e3[me.z] = jnp.sum(e2[...], axis=0)
    spread_z(net, "e3", e3)
    side_z(2)
    swap_queries(2)
    share_basis.relay(2)
    share_basis.relay(3)
    train_y(2)
    side_z(3)
    swap_queries(3)
    share_basis.end()
    multiply(0)
    multiply(1)
    side_z(4)
    swap_queries(4)
    share_eigs.relay(0)
    multiply(2)
    combine(0)
    train_y(3)
    multiply(3)
    combine(1)
    collect_z(net, "e3", e3)
    eig_sum[...] = jnp.sum(e3[...], axis=0)
    damp = (0.1 / (DS * DA)) * jnp.sum(eig_sum[...])
    for back in range(1, GROUP):
        g = step(me.g, -back, GROUP)
        n = (g // 4) * 2 + lax.rem(g, 2)
        net.arrive(qr.at[lax.rem(g // 2, 2), pl.ds(n * rows_q, rows_q)], ("qr", back))
    share_eigs.end()
    inverse[...] = 1.0 / (eigs_all[...].astype(f32) + damp)
    queries = pairs.shape[0]
    lax.fori_loop(0, queries // 2, scale, 0, unroll=2)
    train_y(4)
    multiply(4)
    combine(2)
    combine(3)
    lax.fori_loop(queries // 2, queries, scale, 0, unroll=2)
    combine(4)
    for back in range(Z):
        at = position(back) * rows_g
        start = pl.multiple_of(step(me.z, -back, Z) * rows_g, rows_g)
        ts[:, at : at + rows_g] = sides[:, :, :, pl.ds(start, rows_g)].reshape(-1, rows_g)
    score((0, 1, 2))
    score((3, 4))

    rows = tr.shape[1]
    row = lax.broadcasted_iota(jnp.int32, (rows, 128), 0)
    lane = lax.broadcasted_iota(jnp.int32, (rows, 128), 1)
    place = row // rows_g
    back = jnp.where(place % 2 == 1, (place + 1) // 2, Z - place // 2)
    z = (me.z + Z - back) % Z
    sample = (me.core * Y + (row % rows_g) // RANK) * Z + z
    sums = jnp.dot(
        pairs[...].reshape(-1, rows), jnp.where(lane == sample, 1.0, 0.0),
        preferred_element_type=f32, precision=lax.Precision.HIGHEST,
    )
    f1[me.g] = jnp.sum(sums.reshape(-1, 8, 128), axis=1)
    spread_group(net, "f1", f1)

    collect_group(net, "f1", f1)
    f2[me.y] = jnp.sum(f1[...], axis=0)
    spread_y(net, "f2", f2)
    collect_y(net, "f2", f2)
    f3[me.z] = jnp.sum(f2[...], axis=0)
    spread_z(net, "f3", f3)
    for back_z in range(Z):
        net.arrive(out_side.at[:, step(me.z, -back_z, Z)], ("swap_q", back_z), when=away)

    @pl.when(home)
    def _():
        out_side[...] = sides[:, :, :, cols:]

    collect_z(net, "f3", f3)
    part_sum[...] = jnp.sum(f3[...], axis=0)
    net.finish()


def precond_kernel(out_side, qr, eig_sum, part_sum, eigs, precond, scores, inv):
    turn = pl.program_id(0)
    x_lo = Place().x_lo
    each = precond.shape[0]

    @pl.when(turn == 0)
    def _():
        damp = (0.1 / (DS * DA)) * jnp.sum(eig_sum[...])
        inv[...] = 1.0 / (eigs[...] + damp)
        total = part_sum[:, : scores.shape[1]]
        scores[...] = total / jnp.sqrt(jnp.float32(RANK * DS * DA))

    for sub in range(each):
        query = turn * each + sub
        block = qr[x_lo]
        lane = lax.broadcasted_iota(jnp.int32, block.shape, 1)
        keep = jnp.logical_and(lane >= query * RANK, lane < (query + 1) * RANK)
        left = jnp.where(keep, block, 0.0).astype(jnp.bfloat16)
        precond[sub] = (nt(left, out_side[...]) * inv[...]).astype(jnp.bfloat16)


def precondition(out_side, qr, eig_sum, part_sum, eigs):
    queries = part_sum.shape[0]
    each = 2
    return pl.pallas_call(
        precond_kernel,
        grid=(queries // each,),
        out_shape=(
            jax.ShapeDtypeStruct((queries,) + eigs.shape, jnp.bfloat16),
            jax.ShapeDtypeStruct((queries, 2 * Y * Z), jnp.float32),
        ),
        in_specs=[VMEM] * 5,
        out_specs=(
            pl.BlockSpec((each,) + eigs.shape, lambda q: (q, 0, 0)),
            pl.BlockSpec((queries, 2 * Y * Z), lambda q: (0, 0)),
        ),
        scratch_shapes=[pltpu.VMEM(eigs.shape, jnp.float32)],
        compiler_params=pltpu.CompilerParams(vmem_limit_bytes=12 << 20),
        name="precondition",
    )(out_side, qr, eig_sum, part_sum, eigs)


def influence(train, basis, eigs, train_out, small, query_in, query_out, queries):
    bf16, f32 = jnp.bfloat16, jnp.float32
    rank, coords = train.shape
    block = basis.shape[0]
    wide = small.shape[1]
    width = wide // Y
    rows = Y * Z * rank
    query_rows = query_in.shape[0]
    rows_s = width // Z
    outer = (Z, rank, train_out.shape[1] // Z)
    return pl.pallas_call(
        rotate_kernel,
        out_shape=(
            jax.ShapeDtypeStruct((Y, Z, rows_s, query_rows), bf16),
            jax.ShapeDtypeStruct((2, block, query_rows), f32),
            jax.ShapeDtypeStruct((8, 128), f32),
            jax.ShapeDtypeStruct((queries, 128), f32),
        ),
        in_specs=[ANY] * 7,
        out_specs=[VMEM] * 4,
        scratch_shapes=[
            pltpu.VMEM((2 * block, rows), bf16),
            pltpu.VMEM((Y, Z, rows_s, rows + query_rows), bf16),
            pltpu.VMEM((2,) + eigs.shape, bf16),
            pltpu.VMEM(eigs.shape, bf16),
            pltpu.VMEM((2,) + eigs.shape, f32),
            pltpu.VMEM(train_out.shape, bf16),
            pltpu.VMEM(outer, bf16),
            pltpu.VMEM((queries, 2 * block, wide), bf16),
            pltpu.VMEM((wide, rows), bf16),
            pltpu.VMEM((queries, 8, rows), f32),
            pltpu.VMEM((GROUP, 8, 128), f32),
            pltpu.VMEM((Y, 8, 128), f32),
            pltpu.VMEM((Z, 8, 128), f32),
            pltpu.VMEM((Z, Y, rank, coords), bf16),
            pltpu.VMEM((2, block, coords), bf16),
            pltpu.VMEM((Z, Y) + outer[1:], bf16),
            pltpu.VMEM((2 * Y, small.shape[0], width), bf16),
            pltpu.VMEM((2 * Y * 128, width), bf16),
            pltpu.VMEM(basis.shape, bf16),
            pltpu.VMEM(query_in.shape, bf16),
            pltpu.VMEM((query_rows, 2 * Y * 128), bf16),
            pltpu.VMEM(eigs.shape, f32),
            pltpu.VMEM((2 * block, rows), bf16),
            pltpu.VMEM((X, 2 * block // X, rows), bf16),
            pltpu.VMEM((width, rows), bf16),
            pltpu.VMEM((Z, rows_s, rows), bf16),
            pltpu.VMEM((width, query_rows), f32),
            pltpu.VMEM((Z, rows_s, query_rows), f32),
            pltpu.VMEM((block, query_rows), f32),
            pltpu.VMEM((4, block // 4, query_rows), f32),
            pltpu.VMEM((GROUP, 8, 128), f32),
            pltpu.VMEM((Y, 8, 128), f32),
            pltpu.VMEM((Z, 8, 128), f32),
            pltpu.SemaphoreType.DMA((288,)),
            pltpu.SemaphoreType.DMA((288,)),
            pltpu.SemaphoreType.DMA((9 + 2 * Y,)),
        ],
        compiler_params=pltpu.CompilerParams(
            collective_id=0, has_side_effects=True, vmem_limit_bytes=58 << 20
        ),
        name="influence",
    )(train, basis, eigs, train_out, small, query_in, query_out)


def shards(query_in, query_out, train_in, train_out, basis_in, basis_out, eigvals):
    queries, qrank, coords = query_in.shape
    eigs = eigvals.T
    out_side, qr, eig_sum, part_sum = influence(
        train_in[0], basis_in, eigs, train_out[0], basis_out.T,
        query_in.reshape(queries * qrank, coords),
        query_out.reshape(queries * qrank, query_out.shape[2]), queries,
    )
    precond, scores = precondition(
        out_side.reshape(-1, out_side.shape[3]), qr, eig_sum, part_sum, eigs
    )
    return precond.transpose(0, 2, 1), scores


def solution(mesh):
    placed = (
        P(None, None, "narrow"),
        P(),
        P("wide", None, "narrow"),
        P("wide", None, None),
        P("wide", "narrow"),
        P("narrow", "wide"),
        P("narrow", "wide"),
    )
    return jax.shard_map(
        shards,
        mesh=mesh,
        in_specs=placed,
        out_specs=(P(None, "narrow", "wide"), P()),
        check_vma=False,
    )
```

time: 1090 us -> 182 us (0.17)
  waiting for transfers between devices: 506 us -> 0 us
  blocking collectives: 447 us -> 0 us
  Pallas kernels: 0 us -> 175 us
  local copies, waits for them, and re-layouts: 34.4 us -> 3.41 us
  matrix products: 30.2 us -> 0 us
  starting transfers between devices: 30 us -> 0 us
  other arithmetic: 25.9 us -> 0 us
  between operations: 15.8 us -> 0.67 us
    all_gather x2 -> x0, waiting for transfers between devices: 494 us -> none  [the longest x1 310 us: shards(): train_part = rotate_in(lax.all_gather(train_in, 'wide', axis=0, tiled=True))]
    psum x3 -> x0, blocking collectives: 278 us -> none  [the longest x1 114 us: shards(): eig_total = lax.psum(jnp.sum(eigvals), ('wide', 'narrow'))]
    pallas_call x0 -> x2, Pallas kernels: none -> 175 us  [the longest x1 171 us: influence(): pl.pallas_call(rotate_kernel, out_shape=(jax.ShapeDtypeStruct((Y, Z, rows...]
    unnamed x1 -> x0, blocking collectives: 169 us -> none
    dot_general x12 -> x0, matrix products: 30.2 us -> none  [the longest x11 29 us: contract_last(): lax.dot_general(left_rows, right_rows, (((1,), (1,)), ((), ())), preferre...]
    unnamed x2 -> x0, other arithmetic: 23.5 us -> none
    unnamed x24 -> x10, local copies, waits for them, and re-layouts: 26 us -> 3.41 us
    unnamed x7 -> x0, starting transfers between devices: 16.1 us -> none
  transfers between devices with their start and end apart: 10 -> 0, of which waited for: 4 -> 0; matrix products, arithmetic and copies ran while one was open for 2% -> 0% of each run, Pallas kernels for 0% -> 0%
where the time goes in v1:
time: 182 us; the launch traced here: 179 us
  Pallas kernels  175 us (96%)
  local copies, waits for them, and re-layouts  3.41 us (2%)
    pallas_call x1, Pallas kernels, influence(): pl.pallas_call(rotate_kernel, out_shape=(jax.ShapeDtypeStruct((Y, Z, rows...  171 us

profile of v1, /device:TPU:1, one launch (start us, length us, event | category | flops | bytes accessed | tf_op | source)
XLA Modules:
  0.0 179.2 jit_solution(1327968885767554374)
XLA Ops:
  0.6 0.0 copy-start
  0.6 171.5 %influence.1 = (bf16[4,8,32,256]{3,2,1,0:T(8,128)(2,1)}, f32[2,224,256]{2,1,0:T(8,128)}, f32[8,128]{1,0:T(8,128)}, f32[8,128]{1,0:T(8,128)}) custom-call(bf16[32,3584]{1,0:T(8,128)(2,1)} %bitcast.14, bf16[224,3584]{1,0:T(8,128)(2,1)} %basis.1, f32[224,1024]{1,0:T(8,128)} %bitcast.8, bf16[32,4096]{1,0:T(8,128)(2,1)} %bitcast.13, bf16[64,1024]{1,0:T(8,128)(2,1)} %bitcast.15, ...), custom_call_target="tpu_custom_call" | custom-call | tf_op jit(solution)/shard_map/influence/pallas_call | solution.py:693
  172.1 0.0 copy-done
  172.2 0.0 copy-start.1
  172.2 1.0 copy-done.1
  173.2 0.0 copy-start.2
  173.2 1.0 copy-done.2
  174.2 0.0 copy-start.3
  174.2 0.7 copy-done.3
  174.9 0.0 copy-start.4
  174.9 0.7 copy-done.4
  175.6 3.6 %precondition.1 = (bf16[8,224,1024]{2,1,0:T(8,128)(2,1)}, f32[8,64]{1,0:T(8,128)}) custom-call(bf16[1024,256]{1,0:T(8,128)(2,1)S(1)} %bitcast.10, f32[2,224,256]{2,1,0:T(8,128)S(1)} %copy-done.2, f32[8,128]{1,0:T(8,128)S(1)} %copy-done.3, f32[8,128]{1,0:T(8,128)S(1)} %copy-done.4, f32[224,1024]{1,0:T(8,128)S(1)} %bitcast.9), custom_call_target="tpu_custom_call" | custom-call | tf_op jit(solution)/shard_map/precondition/pallas_call | solution.py:665
Async XLA Ops:
  0.6 171.5 %copy-start = (f32[1024,224]{0,1:T(8,128)S(1)}, f32[1024,224]{0,1:T(8,128)}, u32[]{:S(2)}) copy-start(f32[1024,224]{0,1:T(8,128)} %param.13) | copy-start | bytes 2752516
  172.2 1.0 copy-start.1
  173.2 1.0 copy-start.2
  174.2 0.7 copy-start.3
  174.9 0.7 copy-start.4

commit v2 on v1

--- a/solution.py
+++ b/solution.py
@@ -347,10 +347,19 @@
 
     pl.when(home)(own_copy.wait)
     net.arrive(own_slot, "swap", when=away)
-    trains = Gather(
-        net, "train", train_all,
-        lambda back_y, back_z: (position(back_z), step(me.y, -back_y, Y)), relative=True,
-    )
+    cut = train.shape[1] // 896 * 128
+
+    def spread(name, columns):
+        return Gather(
+            net, name, train_all,
+            lambda back_y, back_z: (
+                position(back_z), step(me.y, -back_y, Y), slice(None), columns
+            ),
+            relative=True,
+        )
+
+    lows = spread("low", slice(0, cut))
+    trains = spread("train", slice(cut, train.shape[1]))
 
     def groups(far):
         return (far,) if far in (0, Z // 2) else (far, -far)
@@ -359,6 +368,9 @@
         trains.ring("z", 0, far, 0)
         for back_z in groups(far):
             trains.ring("y", back_z, 0, back_z)
+        if far > 0:
+            for back in range(Y):
+                lows.ring("z", back, far, back)
 
     def train_y(far):
         for hop in range(1, Y // 2 + 1):
@@ -369,7 +381,9 @@
         for back in range(Y):
             smalls.ring("z", back, far, back)
 
+    lows.direct_y()
     train_z(0)
+    lows.ring("z", 0, 0, 0)
     share_basis = PairShare(net, "basis", basis, basis_all, 4)
     share_eigs = PairShare(net, "eigs", eigs_round, eigs_all, 1)
 
@@ -533,25 +547,28 @@
 
     outer_rows()
     share_basis.start(0)
+    for back in range(1, Y):
+        lows.arrive(back, 0)
+        lows.ring("z", back, 0, back)
     train_z(1)
     query_parts()
+    side_parts()
     train_z(2)
-    side_parts()
-    train_z(3)
     share_basis.start(1)
     query_sums()
     collect_group(net, "e1", e1)
     e2[me.y] = jnp.sum(e1[...], axis=0)
     spread_y(net, "e2", e2)
-    train_z(4)
+    train_z(3)
     share_basis.start(2)
     share_basis.start(3)
+    share_eigs.start(0)
     side_sums()
     smalls.direct_y()
     smalls.ring("z", 0, 0, 0)
+    train_y(0)
+    train_z(4)
     place_own()
-    train_y(0)
-    share_eigs.start(0)
     for back in range(1, Y):
         smalls.arrive(back, 0)
         smalls.ring("z", back, 0, back)
@@ -568,6 +585,7 @@
     swap_queries(2)
     share_basis.relay(2)
     share_basis.relay(3)
+    share_eigs.relay(0)
     train_y(2)
     side_z(3)
     swap_queries(3)
@@ -576,12 +594,8 @@
     multiply(1)
     side_z(4)
     swap_queries(4)
-    share_eigs.relay(0)
     multiply(2)
     combine(0)
-    train_y(3)
-    multiply(3)
-    combine(1)
     collect_z(net, "e3", e3)
     eig_sum[...] = jnp.sum(e3[...], axis=0)
     damp = (0.1 / (DS * DA)) * jnp.sum(eig_sum[...])
@@ -591,19 +605,21 @@
         net.arrive(qr.at[lax.rem(g // 2, 2), pl.ds(n * rows_q, rows_q)], ("qr", back))
     share_eigs.end()
     inverse[...] = 1.0 / (eigs_all[...].astype(f32) + damp)
+    combine(1)
+    train_y(3)
+    multiply(3)
     queries = pairs.shape[0]
-    lax.fori_loop(0, queries // 2, scale, 0, unroll=2)
-    train_y(4)
-    multiply(4)
-    combine(2)
-    combine(3)
-    lax.fori_loop(queries // 2, queries, scale, 0, unroll=2)
-    combine(4)
+    lax.fori_loop(0, queries, scale, 0, unroll=2)
     for back in range(Z):
         at = position(back) * rows_g
         start = pl.multiple_of(step(me.z, -back, Z) * rows_g, rows_g)
         ts[:, at : at + rows_g] = sides[:, :, :, pl.ds(start, rows_g)].reshape(-1, rows_g)
+    combine(2)
+    train_y(4)
+    multiply(4)
+    combine(3)
     score((0, 1, 2))
+    combine(4)
     score((3, 4))
 
     rows = tr.shape[1]

time: 182 us -> 175 us (0.962); the launches traced: 179 us -> 174 us
  Pallas kernels: 175 us -> 170 us
    pallas_call x1, Pallas kernels: 171 us -> 167 us  [influence(): pl.pallas_call(rotate_kernel, out_shape=(jax.ShapeDtypeStruct((Y, Z, rows...]
where the time goes in v2:
time: 175 us; the launch traced here: 174 us
  Pallas kernels  170 us (97%)
  local copies, waits for them, and re-layouts  3.41 us (2%)
    pallas_call x1, Pallas kernels, influence(): pl.pallas_call(rotate_kernel, out_shape=(jax.ShapeDtypeStruct((Y, Z, rows...  167 us
    pallas_call x1, Pallas kernels, precondition(): pl.pallas_call(precond_kernel, grid=(queries // each,), out_shape=(jax.Sh...  3.59 us

profile of v2, /device:TPU:1, one launch (start us, length us, event | category | flops | bytes accessed | tf_op | source)
XLA Modules:
  0.0 174.5 jit_solution(18007362960405443319)
XLA Ops:
  0.6 0.0 copy-start
  0.6 166.8 %influence.1 = (bf16[4,8,32,256]{3,2,1,0:T(8,128)(2,1)}, f32[2,224,256]{2,1,0:T(8,128)}, f32[8,128]{1,0:T(8,128)}, f32[8,128]{1,0:T(8,128)}) custom-call(bf16[32,3584]{1,0:T(8,128)(2,1)} %bitcast.14, bf16[224,3584]{1,0:T(8,128)(2,1)} %basis.1, f32[224,1024]{1,0:T(8,128)} %bitcast.8, bf16[32,4096]{1,0:T(8,128)(2,1)} %bitcast.13, bf16[64,1024]{1,0:T(8,128)(2,1)} %bitcast.15, ...), custom_call_target="tpu_custom_call" | custom-call | tf_op jit(solution)/shard_map/influence/pallas_call | solution.py:709
  167.5 0.0 copy-done
  167.5 0.0 copy-start.1
  167.5 1.0 copy-done.1
  168.5 0.0 copy-start.2
  168.5 1.0 copy-done.2
  169.5 0.0 copy-start.3
  169.5 0.7 copy-done.3
  170.2 0.0 copy-start.4
  170.2 0.7 copy-done.4
  170.9 3.6 %precondition.1 = (bf16[8,224,1024]{2,1,0:T(8,128)(2,1)}, f32[8,64]{1,0:T(8,128)}) custom-call(bf16[1024,256]{1,0:T(8,128)(2,1)S(1)} %bitcast.10, f32[2,224,256]{2,1,0:T(8,128)S(1)} %copy-done.2, f32[8,128]{1,0:T(8,128)S(1)} %copy-done.3, f32[8,128]{1,0:T(8,128)S(1)} %copy-done.4, f32[224,1024]{1,0:T(8,128)S(1)} %bitcast.9), custom_call_target="tpu_custom_call" | custom-call | tf_op jit(solution)/shard_map/precondition/pallas_call | solution.py:681
Async XLA Ops:
  0.6 166.8 %copy-start = (f32[1024,224]{0,1:T(8,128)S(1)}, f32[1024,224]{0,1:T(8,128)}, u32[]{:S(2)}) copy-start(f32[1024,224]{0,1:T(8,128)} %param.13) | copy-start | bytes 2752516
  167.5 1.0 copy-start.1
  168.5 1.0 copy-start.2
  169.5 0.7 copy-start.3
  170.2 0.7 copy-start.4

commit v3 on v2

--- a/solution.py
+++ b/solution.py
@@ -347,7 +347,7 @@
 
     pl.when(home)(own_copy.wait)
     net.arrive(own_slot, "swap", when=away)
-    cut = train.shape[1] // 896 * 128
+    cut = train.shape[1] // 896 * 256
 
     def spread(name, columns):
         return Gather(
@@ -367,15 +367,16 @@
     def train_z(far):
         trains.ring("z", 0, far, 0)
         for back_z in groups(far):
-            trains.ring("y", back_z, 0, back_z)
+            for back in range(1, Y):
+                trains.send("y", 0, back_z, back)
         if far > 0:
             for back in range(Y):
                 lows.ring("z", back, far, back)
 
     def train_y(far):
-        for hop in range(1, Y // 2 + 1):
-            for back_z in groups(far):
-                trains.ring("y", back_z, hop, back_z)
+        for back_z in groups(far):
+            for back in range(1, Y):
+                trains.arrive(back, back_z)
 
     def side_z(far):
         for back in range(Y):

time: 175 us -> 164 us (0.937)
  Pallas kernels: 170 us -> 160 us
    pallas_call x1, Pallas kernels: 167 us -> 156 us  [influence(): pl.pallas_call(rotate_kernel, out_shape=(jax.ShapeDtypeStruct((Y, Z, rows...]
where the time goes in v3:
time: 164 us
  Pallas kernels  160 us (98%)
  local copies, waits for them, and re-layouts  3.41 us (2%)
    pallas_call x1, Pallas kernels, influence(): pl.pallas_call(rotate_kernel, out_shape=(jax.ShapeDtypeStruct((Y, Z, rows...  156 us
    pallas_call x1, Pallas kernels, precondition(): pl.pallas_call(precond_kernel, grid=(queries // each,), out_shape=(jax.Sh...  3.61 us
    unnamed x10, local copies, waits for them, and re-layouts  3.41 us

profile of v3, /device:TPU:1, one launch (start us, length us, event | category | flops | bytes accessed | tf_op | source)
XLA Modules:
  0.0 164.2 jit_solution(16758780805874947225)
XLA Ops:
  0.6 0.0 copy-start
  0.6 156.5 %influence.1 = (bf16[4,8,32,256]{3,2,1,0:T(8,128)(2,1)}, f32[2,224,256]{2,1,0:T(8,128)}, f32[8,128]{1,0:T(8,128)}, f32[8,128]{1,0:T(8,128)}) custom-call(bf16[32,3584]{1,0:T(8,128)(2,1)} %bitcast.14, bf16[224,3584]{1,0:T(8,128)(2,1)} %basis.1, f32[224,1024]{1,0:T(8,128)} %bitcast.8, bf16[32,4096]{1,0:T(8,128)(2,1)} %bitcast.13, bf16[64,1024]{1,0:T(8,128)(2,1)} %bitcast.15, ...), custom_call_target="tpu_custom_call" | custom-call | tf_op jit(solution)/shard_map/influence/pallas_call | solution.py:710
  157.1 0.0 copy-done
  157.1 0.0 copy-start.1
  157.2 1.0 copy-done.1
  158.2 0.0 copy-start.2
  158.2 1.0 copy-done.2
  159.2 0.0 copy-start.3
  159.2 0.7 copy-done.3
  159.9 0.0 copy-start.4
  159.9 0.7 copy-done.4
  160.6 3.6 %precondition.1 = (bf16[8,224,1024]{2,1,0:T(8,128)(2,1)}, f32[8,64]{1,0:T(8,128)}) custom-call(bf16[1024,256]{1,0:T(8,128)(2,1)S(1)} %bitcast.10, f32[2,224,256]{2,1,0:T(8,128)S(1)} %copy-done.2, f32[8,128]{1,0:T(8,128)S(1)} %copy-done.3, f32[8,128]{1,0:T(8,128)S(1)} %copy-done.4, f32[224,1024]{1,0:T(8,128)S(1)} %bitcast.9), custom_call_target="tpu_custom_call" | custom-call | tf_op jit(solution)/shard_map/precondition/pallas_call | solution.py:682
Async XLA Ops:
  0.6 156.5 %copy-start = (f32[1024,224]{0,1:T(8,128)S(1)}, f32[1024,224]{0,1:T(8,128)}, u32[]{:S(2)}) copy-start(f32[1024,224]{0,1:T(8,128)} %param.13) | copy-start | bytes 2752516
  157.1 1.0 copy-start.1
  158.2 1.0 copy-start.2
  159.2 0.7 copy-start.3
  159.9 0.7 copy-start.4
